TPU v7x, 256 devices: a whole 4x4x8 slice. The times are simulated.
256 devices in a mesh: layer: 16 (over x, y), slab: 16 (over z, core).
Axes of the slice: x: 4, y: 4, z: 8, core: 2. Of those that a mesh axis runs over, the one named last changes fastest.
Arguments:
- labels: int32 [32768, 2048], P(('layer', 'slab')), parts along dimension 0, may hold values from 0 to 3
Outputs:
- q_panel: float32 [2, 16384, 20402], P(None, ('layer', 'slab')), parts along dimension 1
There are 16 independent parts, one for each index of `layer`. A program takes and returns all parts, laid end to end along the dimension named above; each array names one. Nothing has to cross between parts.
All inputs are finite; a program needn't handle non-finite values.
Results may differ from a plain program's by a relative error of at most 0.0003.
Values sent between devices are 32-bit elements; how exact they have to be, the bound alone decides.
A program may use at most 192 MiB of HBM per device.

v0:
```python
import math

import jax
import jax.numpy as jnp
from jax import lax
from jax.sharding import PartitionSpec as P

HARM = 101
ROWS_DEV = 64
KEEP = 201
ORDERS = 10201


PERMITS = (1.0, 2.1, 4.0, 12.1)


def extended_2(block, sides, width):
    for axis, dim in sides:
        count = lax.axis_size(axis)
        forward = [(i, i + 1) for i in range(count - 1)]
        forward.append((count - 1, 0))
        backward = [(target, source) for source, target in forward]
        low = lax.ppermute(
            lax.slice_in_dim(block, block.shape[dim] - width, None, axis=dim), axis, forward
        )
        high = lax.ppermute(lax.slice_in_dim(block, 0, width, axis=dim), axis, backward)
        block = jnp.concatenate([low, block, high], axis=dim)
    return block


def permittivity(labels):
    total = jnp.zeros(labels.shape, jnp.float32)
    for index_value in range(4):
        total = total + jnp.where(
            labels == index_value, jnp.float32(PERMITS[index_value]), jnp.float32(0.0)
        )
    return total


def smooth_once(extended):
    middle = extended[1:-1]
    return (
        4.0 * middle
        + extended[:-2]
        + extended[2:]
        + jnp.roll(middle, 1, 1)
        + jnp.roll(middle, -1, 1)
    ) / 8.0


def gradient(extended):
    middle = extended[1:-1]
    grad_x = (extended[2:] - extended[:-2]) / 2.0
    grad_y = (jnp.roll(middle, -1, 1) - jnp.roll(middle, 1, 1)) / 2.0
    return (grad_x, grad_y)


def rim_rows(field_in):
    return extended_2(field_in, (("slab", 0),), 1)


def row_transform(spectra_in, positions, frequency, map_width):
    phases = frequency[:, None] * positions[None, :] % map_width
    angles = phases.astype(jnp.float32) * (2.0 * math.pi / map_width)
    table = jnp.stack([jnp.cos(angles), jnp.sin(angles)])
    products = jnp.einsum("smx,kxcn->skmcn", table, spectra_in, precision=lax.Precision.HIGHEST)
    real_part = products[0, :, :, 0] + products[1, :, :, 1]
    imag_part = products[0, :, :, 1] - products[1, :, :, 0]
    return jnp.stack([real_part, imag_part])


def build_rows(coefficients, window_rows, spacing):
    centre = (HARM - 1) // 2
    order_count = HARM * HARM
    row_count = window_rows.shape[0]
    flipped = coefficients[:, :, ::-1, ::-1]
    order_index = window_rows // 2 * spacing
    lower_half = (window_rows % 2)[:, None]
    first_index = order_index // HARM
    second = order_index % HARM
    zero_start = jnp.zeros((), jnp.int32)

    def cut_window(first_start, second_start):
        return lax.dynamic_slice(
            flipped, (zero_start, zero_start, first_start, second_start), (2, 4, HARM, HARM)
        )

    windows = jax.vmap(cut_window, out_axes=2)(HARM - 1 - first_index, HARM - 1 - second)
    toeplitz = windows.reshape(2, 4, row_count, order_count)
    orders = jnp.arange(order_count, dtype=jnp.int32)
    kx_row = (0.3 + 0.02 * (first_index - centre).astype(jnp.float32))[:, None]
    ky_row = (0.2 + 0.02 * (second - centre).astype(jnp.float32))[:, None]
    diag_real = (orders[None, :] == order_index[:, None]).astype(jnp.float32)
    diag_pair = jnp.stack([diag_real, jnp.zeros_like(diag_real)])
    top_left = kx_row * ky_row * diag_pair + toeplitz[:, 2]
    top_right = toeplitz[:, 0] - toeplitz[:, 3] - kx_row * kx_row * diag_pair
    low_left = ky_row * ky_row * diag_pair - toeplitz[:, 0] + toeplitz[:, 1]
    low_right = -toeplitz[:, 2] - kx_row * ky_row * diag_pair
    upper_row = jnp.concatenate([top_left, top_right], axis=2)
    lower_row = jnp.concatenate([low_left, low_right], axis=2)
    return jnp.where(lower_half[None] == 1, lower_row, upper_row)


def shards(labels):
    slab_rows = labels.shape[0]
    map_width = labels.shape[1]
    devices = lax.axis_size("slab")
    my_index = lax.axis_index("slab")
    permit = permittivity(labels)
    smooth = permit
    for sweep_index in range(3):
        smooth = smooth_once(rim_rows(smooth))
    grad_x, grad_y = gradient(rim_rows(smooth))
    scale = jnp.sqrt(grad_x * grad_x + grad_y * grad_y + 1.0)
    normal_x = grad_x / scale
    normal_y = grad_y / scale
    inverse = 1.0 / permit
    contrast = permit - inverse
    fields = jnp.stack(
        [
            permit,
            contrast * normal_x * normal_x,
            contrast * normal_x * normal_y,
            contrast * normal_y * normal_y,
        ]
    )
    padded_keep = -(-KEEP // devices) * devices
    frequency = jnp.arange(padded_keep, dtype=jnp.int32) - (HARM - 1)
    columns = jnp.arange(map_width, dtype=jnp.int32)
    phases = columns[:, None] * frequency[None, :] % map_width
    angles = phases.astype(jnp.float32) * (2.0 * math.pi / map_width)
    col_table = jnp.stack([jnp.cos(angles), -jnp.sin(angles)], axis=1)
    half_spectra = jnp.einsum("kxy,ycn->kxcn", fields, col_table, precision=lax.Precision.HIGHEST)
    my_positions = my_index * slab_rows + jnp.arange(slab_rows, dtype=jnp.int32)
    partial_value = row_transform(half_spectra, my_positions, frequency, map_width)
    summed = lax.psum(partial_value, "slab")
    coefficients = summed[:, :, :KEEP, :KEEP] / float(map_width * map_width)
    spacing = ORDERS // (ROWS_DEV * devices // 2)
    window_rows = my_index * ROWS_DEV + jnp.arange(ROWS_DEV, dtype=jnp.int32)
    return build_rows(coefficients, window_rows, spacing)


def solution(mesh):
    placed = (P(("layer", "slab"), None),)
    return jax.shard_map(
        shards,
        mesh=mesh,
        in_specs=placed,
        out_specs=P(None, ("layer", "slab"), None),
        check_vma=False,
    )
```

profile of v0, /device:TPU:1, one launch (start us, length us, event | category | flops | bytes accessed | tf_op | source)
XLA Modules:
  0.0 491.0 jit_solution(12071533622216212147)
XLA Ops:
  6.5 1.6 select_add_fusion.1
  8.2 3.0 collective-permute-start
  11.9 8.8 %fusion.42 = (f32[2048,1,208]{0,2,1:T(8,128)}, f32[2048,1,208]{0,2,1:T(8,128)}) fusion(s32[208]{0:T(256)S(1)} %iota_add_fusion), kind=kLoop, calls=%fused_computation.82 | loop fusion | flops 6389760 | bytes 3408704 | tf_op jit(solution)/shard_map/cos | solution.py:132
  22.1 1.5 collective-permute-start.2
  23.6 2.1 collective-permute-start.3
  27.6 3.3 collective-permute-start.5
  32.7 3.5 collective-permute-start.6
  37.0 2.8 collective-permute-done.7
  43.0 5.8 %fusion.19 = f32[4,128,2,208,1]{1,3,4,2,0:T(8,128)S(1)} fusion(f32[2048,1,208]{0,2,1:T(8,128)S(1)} %copy-done.2, f32[2048,1,208]{0,2,1:T(8,128)S(1)} %copy-done.1, f32[1,128,2048]{2,1,0:T(8,128)S(1)} %fusion.20, f32[1,128,2048]{2,1,0:T(8,128)S(1)} %get-tuple-element.35, f32[1,128,2048]{2,1,0:T(8,128)S(1)} %get-tuple-element.33, ...), kind=kOutput, calls=%fused_computation.42 | convolution fusion | flops 5238489088 | bytes 8454144 | tf_op jit(solution)/shard_map/kxy,ycn->kxcn/dot_general | solution.py:133
  48.8 2.8 convolution_bitcast_fusion
  53.9 116.5 %all-reduce.3.cloned.1.call-done = f32[2,4,208,208]{2,3,1,0:T(8,128)} async-done(((f32[2,4,208,208]{2,3,1,0:T(8,128)}), f32[2,4,208,208]{2,3,1,0:T(8,128)}) %all-reduce.3.cloned.1.call-update) | async-done | bytes 1384464 | tf_op jit(solution)/shard_map/psum | solution.py:136
  170.4 17.1 %reverse.4 = f32[2,4,256,208]{2,3,1,0:T(8,128)} reverse(f32[2,4,256,208]{2,3,1,0:T(8,128)} %bitcast.84), dimensions={2,3} | reverse | bytes 3407872
  187.5 2.0 broadcast_multiply_fusion
  189.5 198.7 %while.1 = (s32[]{:T(128)}, f32[2,4,201,201]{2,3,1,0:T(8,128)S(1)}, s32[64,4]{0,1:T(4,128)S(1)}, f32[64,2,4,101,101]{4,3,2,1,0:T(8,128)}, s32[]{:T(128)}) while((s32[]{:T(128)}, f32[2,4,201,201]{2,3,1,0:T(8,128)S(1)}, s32[64,4]{0,1:T(4,128)S(1)}, f32[64,2,4,101,101]{4,3,2,1,0:T(8,128)}, s32[]{:T(128)}) %tuple.50), condition=%wide.while_cond, body=%wide.while_body.sunk | while | flops 2 | bytes 2058777 | solution.py:84
  190.1 1.5 constant_dynamic-slice_fusion.5
  193.2 1.5 constant_dynamic-slice_fusion.5
  202.5 1.5 constant_dynamic-slice_fusion.5
  205.6 1.5 constant_dynamic-slice_fusion.5
  208.7 1.5 constant_dynamic-slice_fusion.5
  214.9 1.5 constant_dynamic-slice_fusion.5
  388.1 27.1 %reshape.525 = f32[2,4,64,10201]{3,1,0,2:T(4,128)} reshape(f32[2,4,64,101,101]{4,3,1,0,2:T(8,128)} %bitcast.83) | data formatting | bytes 41783296 | tf_op jit(solution)/shard_map/reshape | solution.py:89
  415.3 35.2 %fusion.68 = (f32[2,1,64,10201]{3,1,0,2:T(1,128)}, f32[2,1,64,10201]{3,1,0,2:T(1,128)}, f32[2,1,64,10201]{3,1,0,2:T(1,128)}, f32[2,1,64,10201]{3,1,0,2:T(1,128)}) fusion(f32[2,4,64,10201]{3,1,0,2:T(4,128)} %reshape.525), kind=kLoop, calls=%fused_computation.132 | loop fusion | bytes 41783296 | tf_op jit(solution)/shard_map/slice | solution.py:96
  450.5 23.6 %select_add_fusion = (f32[2,64,10201]{2,1,0:T(8,128)S(1)}, f32[2,64,10201]{2,1,0:T(8,128)S(1)}, f32[2,64,10201]{2,1,0:T(8,128)}, f32[2,64,10201]{2,1,0:T(8,128)}) fusion(pred[1,64,10201]{2,1,0:T(8,128)(4,1)S(1)} %iota_compare_fusion, f32[2,1,64,10201]{3,1,0,2:T(1,128)} %get-tuple-element.46, f32[64]{0:T(128)S(1)} %get-tuple-element.85, ...), kind=kLoop, calls=%fused_computation.4 | loop fusion | flops 13057280 | bytes 42436928 | tf_op jit(solution)/shard_map/add | solution.py:95
  474.1 10.1 %maximum_select_fusion = f32[2,64,20402]{2,1,0:T(8,128)} fusion(f32[2,64,10201]{2,1,0:T(8,128)S(1)} %get-tuple-element.48, f32[2,64,10201]{2,1,0:T(8,128)} %get-tuple-element.76, f32[2,64,10201]{2,1,0:T(8,128)} %get-tuple-element.77, f32[2,64,10201]{2,1,0:T(8,128)S(1)} %get-tuple-element.47, pred[64]{0:T(512)(128)(4,1)S(1)} %fusion.50), kind=kLoop, calls=%fused_computation.3 | loop fusion | flops 7834368 | bytes 31337536 | tf_op jit(solution)/shard_map/jit(_where)/select_n | solution.py:101
  (366 shorter events, 201.6 us)
Async XLA Ops:
  6.5 163.9 %all-reduce.3.cloned.1.call-start = ((), (), s32[]{:S(2)}) async-start(), calls=%async_computation | async-start | bytes 3407872 | tf_op jit(solution)/shard_map/psum | solution.py:136
  8.2 13.1 %collective-permute-start = (f32[1,2048]{1,0:T(1,128)S(1)}, f32[1,2048]{1,0:T(1,128)S(1)}, u32[]{:S(2)}, u32[]{:S(2)}) collective-permute-start(f32[1,2048]{1,0:T(1,128)S(1)} %get-tuple-element.70), channel_id=1, source_target_pairs={{0,1},{1,2},{2,3},{3,4},{4,5},{5,6},{6,7},{7,8},{8,9},{9,10},{10,1... | collective-permute-start | bytes 24584 | tf_op jit(solution)/shard_map/ppermute | solution.py:23
  11.2 10.0 %collective-permute-start.1 = (f32[1,2048]{1,0:T(1,128)S(1)}, f32[1,2048]{1,0:T(1,128)S(1)}, u32[]{:S(2)}, u32[]{:S(2)}) collective-permute-start(f32[1,2048]{1,0:T(1,128)S(1)} %get-tuple-element.71), channel_id=1, source_target_pairs={{1,0},{2,1},{3,2},{4,3},{5,4},{6,5},{7,6},{8,7},{9,8},{10,9},{11,1... | collective-permute-start | bytes 24584 | tf_op jit(solution)/shard_map/ppermute | solution.py:26
  22.1 4.2 collective-permute-start.2
  23.6 3.1 collective-permute-start.3
  27.6 4.0 collective-permute-start.4
  27.6 4.1 collective-permute-start.5
  31.8 8.0 %copy-start = (s32[128,2048]{1,0:T(8,128)S(1)}, s32[128,2048]{1,0:T(8,128)}, u32[]{:S(2)}) copy-start(s32[128,2048]{1,0:T(8,128)} %param.1) | copy-start | bytes 3145732
  32.7 4.3 collective-permute-start.6
  36.2 3.6 collective-permute-start.7
  41.1 1.9 copy-start.1
  41.1 2.0 copy-start.2
Sparse Core Ops, SparseCore 0:
  53.4 116.9 all-reduce.2
where the time goes:
time: 494 us; the launch traced here: 491 us
  local copies, waits for them, and re-layouts  280 us (57%)
  waiting for transfers between devices  122 us (25%)
  other arithmetic  53.4 us (11%)
  starting transfers between devices  13.7 us (3%)
  between operations  13.6 us (3%)
  matrix products  8.62 us (2%)
    gather x320, local copies, waits for them, and re-layouts  198 us
    psum x1, waiting for transfers between devices, shards(): summed = lax.psum(partial_value, 'slab')  117 us
    slice x1, local copies, waits for them, and re-layouts, build_rows(): top_right = toeplitz[:, 0] - toeplitz[:, 3] - kx_row * kx_row * diag_pair  35.2 us
    reshape x1, local copies, waits for them, and re-layouts, build_rows(): toeplitz = windows.reshape(2, 4, row_count, order_count)  27.1 us
    add x1, other arithmetic, build_rows(): top_left = kx_row * ky_row * diag_pair + toeplitz[:, 2]  23.6 us
    unnamed x7, local copies, waits for them, and re-layouts  17.2 us
    select_n x1, other arithmetic, build_rows(): return jnp.where(lower_half[None] == 1, lower_row, upper_row)  10.1 us
  transfers between devices with their start and end apart: 9, of which 7 were waited for; matrix products, arithmetic and copies ran while one was open for 2% of the time, Pallas kernels for 0%

commit v1 on v0

v1 whole, which is shorter than its diff:
```python
import jax
import jax.numpy as jnp
import numpy as np
from jax import lax
from jax.experimental import pallas as pl
from jax.experimental.pallas import tpu as pltpu
from jax.sharding import PartitionSpec as P

NMAP = 2048
HARM = 101
ORDERS = HARM * HARM
ROWS_DEV = 64
SLABS = 16
ROWS = NMAP // SLABS
SPACING = ORDERS // (ROWS_DEV * SLABS // 2)
HALF = 104
MAPROWS = 2 * HALF
OWN = 40
EDGE = 8
TOP = 8
EXT = ROWS + 2 * EDGE
PERMITS = (1.0, 2.1, 4.0, 12.1)
MAPS = 3
NTAB = 112


def split_numpy(table):
    high = table.astype(jnp.bfloat16)
    low = (table - high.astype(np.float64)).astype(jnp.bfloat16)
    return high, low


def column_table():
    freq = np.arange(HARM)[:, None]
    angle = 2.0 * np.pi * (freq * np.arange(NMAP)[None, :] % NMAP) / NMAP
    table = np.zeros((MAPROWS, NMAP))
    table[:HARM] = np.cos(angle)
    table[HALF : HALF + HARM] = -np.sin(angle)
    return np.concatenate(split_numpy(table))


def row_table():
    freq = np.arange(HARM)[None, :]
    angle = 2.0 * np.pi * (freq * np.arange(NMAP)[:, None] % NMAP) / NMAP
    table = np.zeros((NMAP, 256))
    table[:, :HARM] = np.cos(angle)
    table[:, 128 : 128 + HARM] = np.sin(angle)
    return np.stack(split_numpy(table / float(NMAP * NMAP)))


def mirror_table():
    table = np.zeros((MAPROWS, 512), np.float32)
    for place in range(2 * HARM - 1):
        n = HARM - 1 - place
        table[abs(n), place] = 1.0
        table[HALF + abs(n), 256 + place] = np.sign(n)
    return table.astype(jnp.bfloat16)


def split(value):
    high = value.astype(jnp.bfloat16)
    low = (value - high.astype(jnp.float32)).astype(jnp.bfloat16)
    return high, low


def dot_f32(a, b, contract):
    return lax.dot_general(a, b, (contract, ((), ())), preferred_element_type=jnp.float32)


def by_label(labels, values):
    low = jnp.where(labels == 0, jnp.float32(values[0]), jnp.float32(values[1]))
    high = jnp.where(labels == 2, jnp.float32(values[2]), jnp.float32(values[3]))
    return jnp.where(labels < 2, low, high)


def spectrum_kernel(
    labels_ref, col_ref, row_ref, out_ref, ext, smooth_a, smooth_b, fields, spec, gathered,
    load_sem, edge_send, edge_recv, spec_send, spec_recv, own_send, own_recv,
):
    me = lax.axis_index("slab")
    before = lax.rem(me + SLABS - 1, SLABS)
    after = lax.rem(me + 1, SLABS)

    load = pltpu.make_async_copy(labels_ref, ext.at[pl.ds(EDGE, ROWS)], load_sem)
    load.start()

    barrier = pltpu.get_barrier_semaphore()
    for step in range(1, SLABS):
        pl.semaphore_signal(barrier, inc=1, device_id={"slab": lax.rem(me + step, SLABS)})
    pl.semaphore_wait(barrier, SLABS - 1)

    up = pltpu.make_async_remote_copy(
        labels_ref.at[pl.ds(0, EDGE)], ext.at[pl.ds(EDGE + ROWS, EDGE)],
        edge_send.at[0], edge_recv.at[0], device_id={"slab": before},
    )
    down = pltpu.make_async_remote_copy(
        labels_ref.at[pl.ds(ROWS - EDGE, EDGE)], ext.at[pl.ds(0, EDGE)],
        edge_send.at[1], edge_recv.at[1], device_id={"slab": after},
    )
    up.start()
    down.start()
    load.wait()
    up.wait()
    down.wait()

    def to_permit(i, carry):
        r = pl.multiple_of(8 * i, 8)
        smooth_a[pl.ds(TOP + r, 8), :] = by_label(ext[pl.ds(r, 8), :], PERMITS)
        return carry

    lax.fori_loop(0, EXT // 8, to_permit, 0)

    def shifted(ref, r, rows):
        prev = ref[pl.ds(r - 8, 8), :]
        mid = ref[pl.ds(r, rows), :]
        nxt = ref[pl.ds(r + rows, 8), :]
        up_ = jnp.concatenate([prev[7:], mid[:-1]], axis=0)
        down_ = jnp.concatenate([mid[1:], nxt[:1]], axis=0)
        return up_, mid, down_

    def smooth_once(src, dst):
        def body(i, carry):
            r = pl.multiple_of(TOP + 8 * i, 8)
            up_, mid, down_ = shifted(src, r, 8)
            side = pltpu.roll(mid, 1, 1) + pltpu.roll(mid, NMAP - 1, 1)
            dst[pl.ds(r, 8), :] = 0.5 * mid + 0.125 * (up_ + down_ + side)
            return carry

        lax.fori_loop(0, EXT // 8, body, 0)

    smooth_once(smooth_a, smooth_b)
    smooth_once(smooth_b, smooth_a)
    smooth_once(smooth_a, smooth_b)

    contrasts = [p - 1.0 / p for p in PERMITS]

    def make_fields(i, carry):
        r = pl.multiple_of(16 * i, 16)
        up_, mid, down_ = shifted(smooth_b, pl.multiple_of(TOP + EDGE + r, 8), 16)
        labels = ext[pl.ds(pl.multiple_of(EDGE + r, 8), 16), :]
        grad_x = 0.5 * (down_ - up_)
        grad_y = 0.5 * (pltpu.roll(mid, NMAP - 1, 1) - pltpu.roll(mid, 1, 1))
        permit = by_label(labels, PERMITS)
        factor = by_label(labels, contrasts) / (grad_x * grad_x + grad_y * grad_y + 1.0)
        along_x = factor * grad_x
        maps = (along_x * grad_y, permit - factor * grad_y * grad_y, along_x * grad_x - permit)
        for k in range(MAPS):
            high, low = split(maps[k])
            fields[k, 0, pl.ds(r, 16), :] = high
            fields[k, 1, pl.ds(r, 16), :] = low
        return carry

    lax.fori_loop(0, ROWS // 16, make_fields, 0)

    for k in range(MAPS):
        product = dot_f32(col_ref[...], fields[k].reshape(2 * ROWS, NMAP), ((1,), (1,)))
        half = product[:, :ROWS] + product[:, ROWS:]
        spec[MAPROWS * k : MAPROWS * (k + 1), :] = half[:MAPROWS] + half[MAPROWS:]
    spec[MAPROWS * MAPS :, :] = jnp.zeros((SLABS * OWN - MAPROWS * MAPS, ROWS), jnp.float32)

    def spec_copy(step):
        to = lax.rem(me + step, SLABS)
        return pltpu.make_async_remote_copy(
            spec.at[pl.ds(pl.multiple_of(to * OWN, 8), OWN)],
            gathered.at[:, pl.ds(pl.multiple_of(me * ROWS, 128), ROWS)],
            spec_send.at[step], spec_recv.at[step], device_id={"slab": to},
        )

    for step in range(1, SLABS):
        spec_copy(step).start()
    mine = pl.ds(pl.multiple_of(me * OWN, 8), OWN)
    gathered[:, pl.ds(pl.multiple_of(me * ROWS, 128), ROWS)] = spec[mine, :]
    for step in range(1, SLABS):
        spec_copy(step).wait()

    high, low = split(gathered[...])
    contract = ((1,), (0,))
    out_ref[mine, :] = (
        dot_f32(high, row_ref[0], contract) + dot_f32(low, row_ref[0], contract) + dot_f32(high, row_ref[1], contract)
    )

    def own_copy(step):
        to = lax.rem(me + step, SLABS)
        return pltpu.make_async_remote_copy(
            out_ref.at[mine], out_ref.at[mine], own_send.at[step], own_recv.at[step], device_id={"slab": to},
        )

    for step in range(1, SLABS):
        own_copy(step).start()
    for step in range(1, SLABS):
        own_copy(step).wait()


def spectrum(labels, col, row):
    vmem = pl.BlockSpec(memory_space=pltpu.VMEM)
    return pl.pallas_call(
        spectrum_kernel,
        out_shape=jax.ShapeDtypeStruct((SLABS * OWN, 256), jnp.float32),
        in_specs=[pl.BlockSpec(memory_space=pl.ANY), vmem, vmem],
        out_specs=vmem,
        scratch_shapes=[
            pltpu.VMEM((EXT, NMAP), jnp.int32),
            pltpu.VMEM((EXT + 2 * TOP, NMAP), jnp.float32),
            pltpu.VMEM((EXT + 2 * TOP, NMAP), jnp.float32),
            pltpu.VMEM((MAPS, 2, ROWS, NMAP), jnp.bfloat16),
            pltpu.VMEM((SLABS * OWN, ROWS), jnp.float32),
            pltpu.VMEM((OWN, NMAP), jnp.float32),
            pltpu.SemaphoreType.DMA,
            pltpu.SemaphoreType.DMA((2,)),
            pltpu.SemaphoreType.DMA((2,)),
            pltpu.SemaphoreType.DMA((SLABS,)),
            pltpu.SemaphoreType.DMA((SLABS,)),
            pltpu.SemaphoreType.DMA((SLABS,)),
            pltpu.SemaphoreType.DMA((SLABS,)),
        ],
        compiler_params=pltpu.CompilerParams(
            collective_id=0, has_side_effects=True, vmem_limit_bytes=40 * 1024 * 1024
        ),
        name="spectrum",
    )(labels, col, row)


def take_lanes(value, index):
    return jnp.take_along_axis(value, index, axis=1, mode="promise_in_bounds")


def build_kernel(me_ref, spec_ref, mirror_ref, out_ref, full, tab):
    group = pl.program_id(0)
    first_order = me_ref[0] * (ROWS_DEV // 2)
    p_last = (first_order + ROWS_DEV // 2 - 1) * SPACING // HARM
    tab_start = HARM - 2 - p_last

    @pl.when(group == 0)
    def make_table():
        mirror = mirror_ref[...]
        for k in range(MAPS):
            high, low = split(spec_ref[MAPROWS * k : MAPROWS * (k + 1), :].T)
            product = dot_f32(high, mirror, ((1,), (0,))) + dot_f32(low, mirror, ((1,), (0,)))
            cos_even, cos_odd = product[:128, :256], product[:128, 256:]
            sin_even, sin_odd = product[128:, :256], product[128:, 256:]
            full[0, k, 0] = cos_even + sin_odd
            full[0, k, 1] = cos_even - sin_odd
            full[1, k, 0] = cos_odd - sin_even
            full[1, k, 1] = cos_odd + sin_even
        odd = lax.broadcasted_iota(jnp.int32, (8, 256), 0) % 2 == 1

        def fill(i, carry):
            m = HARM - 1 - (tab_start + i)
            sign = jnp.where(m < 0, 1, 0)
            row = jnp.minimum(jnp.abs(m), 127)
            for part in range(2):
                rows = [jnp.broadcast_to(full[part, k, sign, pl.ds(row, 1), :], (8, 256)) for k in range(MAPS)]
                tab[part, 0, i] = jnp.where(odd, rows[2], rows[0])
                tab[part, 1, i] = jnp.where(odd, -rows[0], rows[1])
            return carry

        lax.fori_loop(0, HARM + 8, fill, 0)

    lane = lax.broadcasted_iota(jnp.int32, (8, 128), 1)
    sub = lax.broadcasted_iota(jnp.int32, (8, 128), 0)
    t0 = first_order + 4 * group
    p0 = t0 * SPACING // HARM
    order = (t0 + sub // 2) * SPACING
    cross = order >= (p0 + 1) * HARM
    cross_wide = jnp.concatenate([cross, cross], axis=1)
    p = jnp.where(cross, p0 + 1, p0)
    q = order - p * HARM
    offset = HARM - 1 - q
    base = lane + offset
    first = HARM - 1 - p0 - tab_start
    current = [None, None]
    for k in range(2 * HARM):
        half, p_j = k // HARM, k % HARM
        tile, start = divmod(HARM * k, 128)
        index = (base + (128 - start)) & 127
        in_low = index >= offset
        for part in range(2):
            source = jnp.where(cross_wide, tab[part, half, first + p_j - 1], tab[part, half, first + p_j])
            segment = jnp.where(in_low, take_lanes(source[:, :128], index), take_lanes(source[:, 128:], index))
            merged = segment if start == 0 else jnp.where(lane < start, current[part], segment)
            if start + HARM >= 128:
                out_ref[part, :, 128 * tile : 128 * tile + 128] = merged
                current[part] = segment
            else:
                current[part] = merged
    last = 2 * ORDERS // 128 * 128
    for part in range(2):
        out_ref[part, :, last:] = current[part][:, : 2 * ORDERS - last]

    upper = sub % 2 == 0
    kx = 0.3 + 0.02 * (p - HARM // 2).astype(jnp.float32)
    ky = 0.2 + 0.02 * (q - HARM // 2).astype(jnp.float32)
    for half in range(2):
        if half == 0:
            wave = jnp.where(upper, kx * ky, ky * ky)
        else:
            wave = -jnp.where(upper, kx * kx, kx * ky)
        column = (t0 * SPACING + half * ORDERS) // 128 * 128
        place = order + half * ORDERS - column
        for j in range(2):
            lanes = pl.ds(pl.multiple_of(column + 128 * j, 128), 128)
            out_ref[0, :, lanes] = out_ref[0, :, lanes] + jnp.where(place == lane + 128 * j, wave, 0.0)


def build(me, spec, mirror):
    return pl.pallas_call(
        build_kernel,
        out_shape=jax.ShapeDtypeStruct((2, ROWS_DEV, 2 * ORDERS), jnp.float32),
        grid_spec=pltpu.PrefetchScalarGridSpec(
            num_scalar_prefetch=1,
            grid=(ROWS_DEV // 8,),
            in_specs=[
                pl.BlockSpec((SLABS * OWN, 256), lambda g, m: (0, 0)),
                pl.BlockSpec((MAPROWS, 512), lambda g, m: (0, 0)),
            ],
            out_specs=pl.BlockSpec((2, 8, 2 * ORDERS), lambda g, m: (0, g, 0)),
            scratch_shapes=[
                pltpu.VMEM((2, MAPS, 2, 128, 256), jnp.float32),
                pltpu.VMEM((2, 2, NTAB, 8, 256), jnp.float32),
            ],
        ),
        compiler_params=pltpu.CompilerParams(vmem_limit_bytes=32 * 1024 * 1024),
        name="build",
    )(me, spec, mirror)


def shards(labels):
    me = lax.axis_index("slab").astype(jnp.int32).reshape(1)
    spec = spectrum(labels, jnp.asarray(column_table()), jnp.asarray(row_table()))
    return build(me, spec, jnp.asarray(mirror_table()))


def solution(mesh):
    return jax.shard_map(
        shards,
        mesh=mesh,
        in_specs=(P(("layer", "slab"), None),),
        out_specs=P(None, ("layer", "slab"), None),
        check_vma=False,
    )
```

time: 494 us -> 68.3 us (0.14)
  local copies, waits for them, and re-layouts: 280 us -> 4.27 us
  waiting for transfers between devices: 122 us -> 0 us
  Pallas kernels: 0 us -> 63.7 us
  other arithmetic: 53.4 us -> 0 us
  starting transfers between devices: 13.7 us -> 0 us
  between operations: 13.6 us -> 0.02 us
  matrix products: 8.62 us -> 0 us
    gather x320 -> x0, local copies, waits for them, and re-layouts: 198 us -> none
    psum x1 -> x0, waiting for transfers between devices: 117 us -> none  [shards(): summed = lax.psum(partial_value, 'slab')]
    pallas_call x0 -> x2, Pallas kernels: none -> 63.7 us  [the longest x1 47.6 us: spectrum(): pl.pallas_call(spectrum_kernel, out_shape=jax.ShapeDtypeStruct((SLABS * O...]
    slice x13 -> x0, local copies, waits for them, and re-layouts: 37 us -> none  [the longest x1 35.2 us: build_rows(): top_right = toeplitz[:, 0] - toeplitz[:, 3] - kx_row * kx_row * diag_pair]
    reshape x1 -> x0, local copies, waits for them, and re-layouts: 27.1 us -> none  [build_rows(): toeplitz = windows.reshape(2, 4, row_count, order_count)]
    add x4 -> x0, other arithmetic: 25.3 us -> none  [the longest x1 23.6 us: build_rows(): top_left = kx_row * ky_row * diag_pair + toeplitz[:, 2]]
    ppermute x8 -> x0, starting transfers between devices: 13.7 us -> none  [the longest x4 9.09 us: extended_2(): lax.ppermute(lax.slice_in_dim(block, 0, width, axis=dim), axis, backward)]
    unnamed x7 -> x8, local copies, waits for them, and re-layouts: 17.2 us -> 4.27 us
  transfers between devices with their start and end apart: 9 -> 0, of which waited for: 7 -> 0; matrix products, arithmetic and copies ran while one was open for 2% -> 0% of each run, Pallas kernels for 0% -> 0%
where the time goes in v1:
time: 68.3 us; the launch traced here: 68 us
  Pallas kernels  63.7 us (93%)
  local copies, waits for them, and re-layouts  4.27 us (6%)
    pallas_call x1, Pallas kernels, spectrum(): pl.pallas_call(spectrum_kernel, out_shape=jax.ShapeDtypeStruct((SLABS * O...  47.6 us
    pallas_call x1, Pallas kernels, build(): pl.pallas_call(build_kernel, out_shape=jax.ShapeDtypeStruct((2, ROWS_DEV,...  16.1 us
    unnamed x8, local copies, waits for them, and re-layouts  4.27 us

profile of v1, /device:TPU:1, one launch (start us, length us, event | category | flops | bytes accessed | tf_op | source)
XLA Modules:
  0.0 68.0 jit_solution(6593242721779688096)
XLA Ops:
  0.0 0.0 copy-start
  0.0 1.6 %copy-done = bf16[2,2048,256]{2,1,0:T(8,128)(2,1)S(1)} copy-done((bf16[2,2048,256]{2,1,0:T(8,128)(2,1)S(1)}, bf16[2,2048,256]{2,1,0:T(8,128)(2,1)}, u32[]{:S(2)}) %copy-start) | copy-done | bytes 2097176
  1.6 0.0 copy-start.1
  1.6 1.5 %copy-done.1 = bf16[416,2048]{1,0:T(8,128)(2,1)S(1)} copy-done((bf16[416,2048]{1,0:T(8,128)(2,1)S(1)}, bf16[416,2048]{1,0:T(8,128)(2,1)}, u32[]{:S(2)}) %copy-start.1) | copy-done | bytes 1703960
  3.0 0.0 copy-start.2
  3.0 1.2 %copy-done.2 = s32[128,2048]{1,0:T(8,128)S(1)} copy-done((s32[128,2048]{1,0:T(8,128)S(1)}, s32[128,2048]{1,0:T(8,128)}, u32[]{:S(2)}) %copy-start.2) | copy-done | bytes 1048600
  4.3 0.0 copy-start.3
  4.3 47.6 %spectrum.1.spec_ref = f32[640,256]{1,0:T(8,128)S(1)} custom-call(s32[128,2048]{1,0:T(8,128)S(1)} %copy-done.2, bf16[416,2048]{1,0:T(8,128)(2,1)S(1)} %copy-done.1, bf16[2,2048,256]{2,1,0:T(8,128)(2,1)S(1)} %copy-done), custom_call_target="tpu_custom_call" | custom-call | tf_op jit(solution)/shard_map/spectrum/pallas_call | solution.py:196
  51.9 0.0 copy-done.3
  51.9 16.1 %build.1 = f32[2,64,20402]{2,1,0:T(8,128)} custom-call(s32[1]{0:T(128)} %bitcast.me_ref, f32[640,256]{1,0:T(8,128)S(1)} %spectrum.1.spec_ref, bf16[208,512]{1,0:T(8,128)(2,1)S(1)} %copy-done.3), custom_call_target="tpu_custom_call" | custom-call | tf_op jit(solution)/shard_map/build/pallas_call | solution.py:306
Async XLA Ops:
  0.0 1.6 %copy-start = (bf16[2,2048,256]{2,1,0:T(8,128)(2,1)S(1)}, bf16[2,2048,256]{2,1,0:T(8,128)(2,1)}, u32[]{:S(2)}) copy-start(bf16[2,2048,256]{2,1,0:T(8,128)(2,1)} %constant.11.clone.row_ref) | copy-start | bytes 6291460
  1.6 1.5 %copy-start.1 = (bf16[416,2048]{1,0:T(8,128)(2,1)S(1)}, bf16[416,2048]{1,0:T(8,128)(2,1)}, u32[]{:S(2)}) copy-start(bf16[416,2048]{1,0:T(8,128)(2,1)} %constant.10.clone.col_ref) | copy-start | bytes 5111812
  3.0 1.2 %copy-start.2 = (s32[128,2048]{1,0:T(8,128)S(1)}, s32[128,2048]{1,0:T(8,128)}, u32[]{:S(2)}) copy-start(s32[128,2048]{1,0:T(8,128)} %labels_ref.1) | copy-start | bytes 3145732
  4.3 47.6 %copy-start.3 = (bf16[208,512]{1,0:T(8,128)(2,1)S(1)}, bf16[208,512]{1,0:T(8,128)(2,1)}, u32[]{:S(2)}) copy-start(bf16[208,512]{1,0:T(8,128)(2,1)} %constant.12.clone.mirror_ref) | copy-start | bytes 638980

commit v2 on v1

v2 whole, which is shorter than its diff:
```python
import jax
import jax.numpy as jnp
import numpy as np
from jax import lax
from jax.experimental import pallas as pl
from jax.experimental.pallas import tpu as pltpu
from jax.sharding import PartitionSpec as P

NMAP = 2048
HARM = 101
ORDERS = HARM * HARM
ROWS_DEV = 64
SLABS = 16
ROWS = NMAP // SLABS
SPACING = ORDERS // (ROWS_DEV * SLABS // 2)
HALF = 104
MAPROWS = 2 * HALF
OWN = 40
EDGE = 8
TOP = 8
EXT = ROWS + 2 * EDGE
PERMITS = (1.0, 2.1, 4.0, 12.1)
MAPS = 3
TABLE = 112
LEAD = 8
PITCH = 9
STRIPS = NMAP // 128
CHIPS = SLABS // 2
EARLY = 24


def split_numpy(table):
    high = table.astype(jnp.bfloat16)
    low = (table - high.astype(np.float64)).astype(jnp.bfloat16)
    return high, low


def column_table():
    freq = np.arange(HARM)[:, None]
    angle = 2.0 * np.pi * (freq * np.arange(NMAP)[None, :] % NMAP) / NMAP
    table = np.zeros((MAPROWS, NMAP))
    table[:HARM] = np.cos(angle)
    table[HALF : HALF + HARM] = -np.sin(angle)
    return np.concatenate(split_numpy(table))


def row_table():
    freq = np.arange(HARM)[None, :]
    angle = 2.0 * np.pi * (freq * np.arange(NMAP)[:, None] % NMAP) / NMAP
    table = np.zeros((NMAP, 256))
    table[:, :HARM] = np.cos(angle)
    table[:, 128 : 128 + HARM] = np.sin(angle)
    return np.stack(split_numpy(table / float(NMAP * NMAP)))


def split(value):
    high = value.astype(jnp.bfloat16)
    low = (value - high.astype(jnp.float32)).astype(jnp.bfloat16)
    return high, low


def dot_f32(a, b, contract):
    return lax.dot_general(a, b, (contract, ((), ())), preferred_element_type=jnp.float32)


def by_label(labels, values):
    low = jnp.where(labels == 0, jnp.float32(values[0]), jnp.float32(values[1]))
    high = jnp.where(labels == 2, jnp.float32(values[2]), jnp.float32(values[3]))
    return jnp.where(labels < 2, low, high)


def spectrum_kernel(
    labels_ref, col_hbm, row_hbm, out_ref, ext, smooth_a, smooth_b, fields, spec, gathered, col_ref, row_ref,
    load_sem, edge_send, edge_recv, spec_send, spec_recv, own_send, own_recv,
):
    me = lax.axis_index("slab")
    before = lax.rem(me + SLABS - 1, SLABS)
    after = lax.rem(me + 1, SLABS)

    load = pltpu.make_async_copy(labels_ref, ext.at[pl.ds(EDGE, ROWS)], load_sem.at[0])
    load.start()
    load_col = pltpu.make_async_copy(col_hbm, col_ref, load_sem.at[1])
    load_row = pltpu.make_async_copy(row_hbm, row_ref, load_sem.at[2])

    barrier = pltpu.get_barrier_semaphore()
    for step in range(1, SLABS):
        pl.semaphore_signal(barrier, inc=1, device_id={"slab": lax.rem(me + step, SLABS)})
    pl.semaphore_wait(barrier, SLABS - 1)

    up = pltpu.make_async_remote_copy(
        labels_ref.at[pl.ds(0, EDGE)], ext.at[pl.ds(EDGE + ROWS, EDGE)],
        edge_send.at[0], edge_recv.at[0], device_id={"slab": before},
    )
    down = pltpu.make_async_remote_copy(
        labels_ref.at[pl.ds(ROWS - EDGE, EDGE)], ext.at[pl.ds(0, EDGE)],
        edge_send.at[1], edge_recv.at[1], device_id={"slab": after},
    )
    up.start()
    down.start()
    load_col.start()
    load_row.start()

    def over_tiles(body, count, skip_at=None, skip=0, first=0):
        def step(i, carry):
            body(first + i if skip_at is None else first + i + jnp.where(i >= skip_at, skip, 0))
            return carry

        lax.fori_loop(0, count, step, 0)

    def to_permit(tile):
        r = pl.multiple_of(8 * tile, 8)
        for j in range(STRIPS):
            smooth_a[j, pl.ds(TOP + r, 8), :] = by_label(ext[pl.ds(r, 8), 128 * j : 128 * (j + 1)], PERMITS)

    def sides(mid, rows):
        lane = lax.broadcasted_iota(jnp.int32, (STRIPS, rows, 128), 2)
        flat = mid.reshape(STRIPS * rows, 128)
        ahead = pltpu.roll(flat, 127, 1).reshape(STRIPS, rows, 128)
        behind = pltpu.roll(flat, 1, 1).reshape(STRIPS, rows, 128)
        ahead = jnp.where(lane == 127, jnp.concatenate([ahead[1:], ahead[:1]], axis=0), ahead)
        behind = jnp.where(lane == 0, jnp.concatenate([behind[-1:], behind[:-1]], axis=0), behind)
        return behind, ahead

    def smooth_tile(src, dst):
        def body(tile):
            r = pl.multiple_of(TOP + 8 * tile, 8)
            mid = src[:, pl.ds(r, 8), :]
            behind, ahead = sides(mid, 8)
            around = src[:, pl.ds(r - 1, 8), :] + src[:, pl.ds(r + 1, 8), :] + behind + ahead
            dst[:, pl.ds(r, 8), :] = 0.5 * mid + 0.125 * around

        return body

    contrasts = [p - 1.0 / p for p in PERMITS]

    def make_fields(block):
        r = pl.multiple_of(16 * block, 16)
        at = pl.multiple_of(TOP + EDGE + r, 8)
        behind, ahead = sides(smooth_b[:, pl.ds(at, 16), :], 16)
        grad_x = 0.5 * (smooth_b[:, pl.ds(at + 1, 16), :] - smooth_b[:, pl.ds(at - 1, 16), :])
        grad_y = 0.5 * (ahead - behind)
        for j in range(STRIPS):
            lanes = slice(128 * j, 128 * (j + 1))
            labels = ext[pl.ds(pl.multiple_of(EDGE + r, 8), 16), lanes]
            permit = by_label(labels, PERMITS)
            gx, gy = grad_x[j], grad_y[j]
            factor = by_label(labels, contrasts) / (gx * gx + gy * gy + 1.0)
            along_x = factor * gx
            maps = (along_x * gy, permit - factor * gy * gy, along_x * gx - permit)
            for k in range(MAPS):
                high, low = split(maps[k])
                fields[k, 0, pl.ds(r, 16), lanes] = high
                fields[k, 1, pl.ds(r, 16), lanes] = low

    load.wait()
    over_tiles(to_permit, 16, first=1)
    over_tiles(smooth_tile(smooth_a, smooth_b), 14, first=2)
    over_tiles(smooth_tile(smooth_b, smooth_a), 12, first=3)
    over_tiles(smooth_tile(smooth_a, smooth_b), 10, first=4)
    over_tiles(make_fields, 4, first=2)
    up.wait()
    down.wait()
    over_tiles(to_permit, 2, 1, 16)
    over_tiles(smooth_tile(smooth_a, smooth_b), 4, 2, 14)
    over_tiles(smooth_tile(smooth_b, smooth_a), 6, 3, 12)
    over_tiles(smooth_tile(smooth_a, smooth_b), 8, 4, 10)
    over_tiles(make_fields, 4, 2, 4)

    load_col.wait()
    for k in range(MAPS):
        product = dot_f32(col_ref[...], fields[k].reshape(2 * ROWS, NMAP), ((1,), (1,)))
        half = product[:, :ROWS] + product[:, ROWS:]
        spec[MAPROWS * k : MAPROWS * (k + 1), :] = half[:MAPROWS] + half[MAPROWS:]
    spec[MAPROWS * MAPS :, :] = jnp.zeros((SLABS * OWN - MAPROWS * MAPS, ROWS), jnp.float32)

    def spec_copy(step):
        to = lax.rem(me + step, SLABS)
        return pltpu.make_async_remote_copy(
            spec.at[pl.ds(pl.multiple_of(to * OWN, 8), OWN)],
            gathered.at[:, pl.ds(pl.multiple_of(me * ROWS, 128), ROWS)],
            spec_send.at[step], spec_recv.at[step], device_id={"slab": to},
        )

    for step in range(1, SLABS):
        spec_copy(step).start()
    mine = pl.ds(pl.multiple_of(me * OWN, 8), OWN)
    gathered[:, pl.ds(pl.multiple_of(me * ROWS, 128), ROWS)] = spec[mine, :]
    load_row.wait()
    for step in range(1, SLABS):
        spec_copy(step).wait()

    high, low = split(gathered[...])
    contract = ((1,), (0,))
    out_ref[mine, :] = (
        dot_f32(high, row_ref[0], contract) + dot_f32(low, row_ref[0], contract) + dot_f32(high, row_ref[1], contract)
    )

    core = lax.rem(me, 2)
    chip = lax.div(me, 2)

    def ship(slot, origin, to, sibling=False, first=0, count=OWN):
        start = (2 * lax.rem(chip + origin + CHIPS, CHIPS) + core) * OWN + first
        rows = out_ref.at[pl.ds(pl.multiple_of(start, 8), count)]
        target = me + 1 - 2 * core if sibling else 2 * lax.rem(chip + to + CHIPS, CHIPS) + core
        return pltpu.make_async_remote_copy(
            rows, rows, own_send.at[slot], own_recv.at[slot], device_id={"slab": target}
        )

    up_part, down_part = dict(first=0, count=EARLY), dict(first=EARLY, count=OWN - EARLY)
    chips = [ship(0, 0, 2), ship(1, 0, -2), ship(2, 0, 1), ship(3, 0, -1),
             ship(4, -2, 2, **up_part), ship(5, 2, -2, **down_part), ship(6, -2, 1), ship(7, 2, -1)]
    siblings = [ship(8, -2, 0, True), ship(9, 2, 0, True), ship(10, -1, 0, True), ship(11, 1, 0, True),
                ship(12, 4, 0, True, **up_part), ship(13, 4, 0, True, **down_part),
                ship(14, -3, 0, True), ship(15, 3, 0, True), ship(16, 0, 0, True)]
    for i in range(4):
        chips[i].start()
    siblings[8].start()
    for i in range(2):
        chips[i].wait_recv()
        chips[4 + i].start()
        chips[6 + i].start()
        siblings[i].start()
    for i in range(2, 8):
        chips[i].wait_recv()
        siblings[i].start()
    for copy in chips:
        copy.wait_send()
    for copy in siblings:
        copy.wait()


def spectrum(labels, col, row):
    vmem = pl.BlockSpec(memory_space=pltpu.VMEM)
    hbm = pl.BlockSpec(memory_space=pltpu.HBM)
    return pl.pallas_call(
        spectrum_kernel,
        out_shape=jax.ShapeDtypeStruct((SLABS * OWN, 256), jnp.float32),
        in_specs=[hbm, hbm, hbm],
        out_specs=vmem,
        scratch_shapes=[
            pltpu.VMEM((EXT, NMAP), jnp.int32),
            pltpu.VMEM((STRIPS, EXT + 2 * TOP, 128), jnp.float32),
            pltpu.VMEM((STRIPS, EXT + 2 * TOP, 128), jnp.float32),
            pltpu.VMEM((MAPS, 2, ROWS, NMAP), jnp.bfloat16),
            pltpu.VMEM((SLABS * OWN, ROWS), jnp.float32),
            pltpu.VMEM((OWN, NMAP), jnp.float32),
            pltpu.VMEM((2 * MAPROWS, NMAP), jnp.bfloat16),
            pltpu.VMEM((2, NMAP, 256), jnp.bfloat16),
            pltpu.SemaphoreType.DMA((3,)),
            pltpu.SemaphoreType.DMA((2,)),
            pltpu.SemaphoreType.DMA((2,)),
            pltpu.SemaphoreType.DMA((SLABS,)),
            pltpu.SemaphoreType.DMA((SLABS,)),
            pltpu.SemaphoreType.DMA((17,)),
            pltpu.SemaphoreType.DMA((17,)),
        ],
        compiler_params=pltpu.CompilerParams(
            collective_id=0, has_side_effects=True, vmem_limit_bytes=63 * 1024 * 1024
        ),
        name="spectrum",
    )(labels, col, row)


def sign_of(value):
    return jnp.where(value > 0, 1.0, jnp.where(value < 0, -1.0, 0.0))


def build_kernel(me_ref, spec_ref, out_ref, toeplitz, windows):
    group = pl.program_id(0)
    first_order = me_ref[0] * (ROWS_DEV // 2)
    p_last = (first_order + ROWS_DEV // 2 - 1) * SPACING // HARM

    @pl.when(group == 0)
    def make_table():
        row = lax.broadcasted_iota(jnp.int32, (2 * TABLE, 256), 0)
        lane = lax.broadcasted_iota(jnp.int32, (2 * TABLE, 256), 1)
        m = p_last - jnp.where(row < TABLE, row, row - TABLE)
        from_cos = jnp.where(lane == jnp.abs(m), 1.0, 0.0)
        from_sin = jnp.where(lane == 128 + jnp.abs(m), sign_of(m), 0.0)
        pick = jnp.where(row < TABLE, from_cos, from_sin).astype(jnp.bfloat16)
        row = lax.broadcasted_iota(jnp.int32, (MAPROWS, 512), 0)
        lane = lax.broadcasted_iota(jnp.int32, (MAPROWS, 512), 1)
        n = HARM - 1 - (lane & 255)
        size = jnp.where(n >= 1 - HARM, jnp.abs(n), MAPROWS)
        even = jnp.where(row == size, 1.0, 0.0)
        uneven = jnp.where(row - HALF == size, sign_of(n), 0.0)
        mirror = jnp.where(lane < 256, even, uneven).astype(jnp.bfloat16)
        for k in range(MAPS):
            high, low = split(spec_ref[MAPROWS * k : MAPROWS * (k + 1), :])
            high, low = split(dot_f32(pick, high, ((1,), (1,))) + dot_f32(pick, low, ((1,), (1,))))
            product = dot_f32(high, mirror, ((1,), (0,))) + dot_f32(low, mirror, ((1,), (0,)))
            cos_rows, sin_rows = product[:TABLE], product[TABLE:]
            real = cos_rows[:, :256] + sin_rows[:, 256:]
            imag = cos_rows[:, 256:] - sin_rows[:, :256]
            for part, value in enumerate((real, imag)):
                rows = pl.ds((part * MAPS + k) * TABLE, TABLE)
                toeplitz[rows, :256], toeplitz[rows, 256:] = split(value)

    t0 = first_order + 4 * group
    row = lax.broadcasted_iota(jnp.int32, (512, 256), 0) & 255
    lane = lax.broadcasted_iota(jnp.int32, (512, 256), 1)
    for pair in range(2):
        orders = [(t0 + 2 * pair + j) * SPACING for j in range(2)]
        p_pair = [order // HARM for order in orders]
        q_pair = [order - p * HARM for order, p in zip(orders, p_pair)]
        source = jnp.where(lane < 128, lane - q_pair[0], lane - 128 - q_pair[1]) + HARM - 1
        shift = jnp.where(row == source, 1.0, 0.0).astype(jnp.bfloat16)
        moved = dot_f32(toeplitz[...], shift, ((1,), (0,)))
        for j in range(2):
            top = (LEAD - (p_last - p_pair[j])) * PITCH + 4 * pair + 2 * j
            for part in range(2):
                cross_xy, right_up, left_low = (
                    moved[(part * MAPS + k) * TABLE : (part * MAPS + k + 1) * TABLE, 128 * j : 128 * j + 128]
                    for k in range(MAPS)
                )
                upper = pl.ds(top, TABLE, stride=PITCH)
                lower = pl.ds(top + 1, TABLE, stride=PITCH)
                windows[part, 0, upper, :] = cross_xy
                windows[part, 0, lower, :] = left_low
                windows[part, 1, upper, :] = right_up
                windows[part, 1, lower, :] = -cross_xy

    lane = lax.broadcasted_iota(jnp.int32, (8, 128), 1)
    sub = lax.broadcasted_iota(jnp.int32, (8, 128), 0)
    current = [None, None]
    for k in range(2 * HARM):
        half, p_j = divmod(k, HARM)
        tile, start = divmod(HARM * k, 128)
        for part in range(2):
            segment = windows[part, half, (LEAD + p_j) * PITCH : (LEAD + p_j) * PITCH + 8, :]
            if start:
                segment = pltpu.roll(segment, start, 1)
                merged = jnp.where(lane < start, current[part], segment)
            else:
                merged = segment
            if start + HARM >= 128:
                out_ref[part, :, 128 * tile : 128 * tile + 128] = merged
                current[part] = segment
            else:
                current[part] = merged
    last = 2 * ORDERS // 128 * 128
    for part in range(2):
        out_ref[part, :, last:] = current[part][:, : 2 * ORDERS - last]

    order = (t0 + sub // 2) * SPACING
    p0 = t0 * SPACING // HARM
    p = jnp.where(order >= (p0 + 1) * HARM, p0 + 1, p0)
    q = order - p * HARM
    upper = sub % 2 == 0
    kx = 0.3 + 0.02 * (p - HARM // 2).astype(jnp.float32)
    ky = 0.2 + 0.02 * (q - HARM // 2).astype(jnp.float32)
    for half in range(2):
        if half == 0:
            wave = jnp.where(upper, kx * ky, ky * ky)
        else:
            wave = -jnp.where(upper, kx * kx, kx * ky)
        column = (t0 * SPACING + half * ORDERS) // 128 * 128
        place = order + half * ORDERS - column
        for j in range(2):
            lanes = pl.ds(pl.multiple_of(column + 128 * j, 128), 128)
            out_ref[0, :, lanes] = out_ref[0, :, lanes] + jnp.where(place == lane + 128 * j, wave, 0.0)


def build(me, spec):
    return pl.pallas_call(
        build_kernel,
        out_shape=jax.ShapeDtypeStruct((2, ROWS_DEV, 2 * ORDERS), jnp.float32),
        grid_spec=pltpu.PrefetchScalarGridSpec(
            num_scalar_prefetch=1,
            grid=(ROWS_DEV // 8,),
            in_specs=[pl.BlockSpec((SLABS * OWN, 256), lambda g, m: (0, 0))],
            out_specs=pl.BlockSpec((2, 8, 2 * ORDERS), lambda g, m: (0, g, 0)),
            scratch_shapes=[
                pltpu.VMEM((2 * MAPS * TABLE, 512), jnp.bfloat16),
                pltpu.VMEM((2, 2, (LEAD + TABLE) * PITCH, 128), jnp.float32),
            ],
        ),
        compiler_params=pltpu.CompilerParams(vmem_limit_bytes=63 * 1024 * 1024),
        name="build",
    )(me, spec)


def shards(labels):
    me = lax.axis_index("slab").astype(jnp.int32).reshape(1)
    spec = spectrum(labels, jnp.asarray(column_table()), jnp.asarray(row_table()))
    return build(me, spec)


def solution(mesh):
    return jax.shard_map(
        shards,
        mesh=mesh,
        in_specs=(P(("layer", "slab"), None),),
        out_specs=P(None, ("layer", "slab"), None),
        check_vma=False,
    )
```

time: 68.3 us -> 52.1 us (0.76)
  Pallas kernels: 63.7 us -> 52 us
  local copies, waits for them, and re-layouts: 4.27 us -> 0 us
    pallas_call x1, Pallas kernels: 47.6 us -> 39.7 us  [spectrum(): pl.pallas_call(spectrum_kernel, out_shape=jax.ShapeDtypeStruct((SLABS * O...]
    unnamed x8 -> x0, local copies, waits for them, and re-layouts: 4.27 us -> none
    pallas_call x1, Pallas kernels: 16.1 us -> 12.2 us  [build(): pl.pallas_call(build_kernel, out_shape=jax.ShapeDtypeStruct((2, ROWS_DEV,...]
where the time goes in v2:
time: 52.1 us; the launch traced here: 52 us
  Pallas kernels  52 us (100%)
    pallas_call x1, Pallas kernels, spectrum(): pl.pallas_call(spectrum_kernel, out_shape=jax.ShapeDtypeStruct((SLABS * O...  39.7 us
    pallas_call x1, Pallas kernels, build(): pl.pallas_call(build_kernel, out_shape=jax.ShapeDtypeStruct((2, ROWS_DEV,...  12.2 us

profile of v2, /device:TPU:1, one launch (start us, length us, event | category | flops | bytes accessed | tf_op | source)
XLA Modules:
  0.0 52.0 jit_solution(2134826589748008620)
XLA Ops:
  0.0 39.7 %spectrum.1.spec_ref = f32[640,256]{1,0:T(8,128)} custom-call(s32[128,2048]{1,0:T(8,128)} %labels_ref.1, bf16[416,2048]{1,0:T(8,128)(2,1)} %constant.8.clone.col_hbm, bf16[2,2048,256]{2,1,0:T(8,128)(2,1)} %constant.9.clone.row_hbm), custom_call_target="tpu_custom_call" | custom-call | tf_op jit(solution)/shard_map/spectrum/pallas_call | solution.py:235
  39.7 12.2 %build.1 = f32[2,64,20402]{2,1,0:T(8,128)} custom-call(s32[1]{0:T(128)} %bitcast.me_ref, f32[640,256]{1,0:T(8,128)} %spectrum.1.spec_ref), custom_call_target="tpu_custom_call" | custom-call | tf_op jit(solution)/shard_map/build/pallas_call | solution.py:365

commit v3 on v2

v3 whole, which is shorter than its diff:
```python
import jax
import jax.numpy as jnp
import numpy as np
from jax import lax
from jax.experimental import pallas as pl
from jax.experimental.pallas import tpu as pltpu
from jax.sharding import PartitionSpec as P

NMAP = 2048
HARM = 101
ORDERS = HARM * HARM
ROWS_DEV = 64
SLABS = 16
ROWS = NMAP // SLABS
SPACING = ORDERS // (ROWS_DEV * SLABS // 2)
HALF = 104
MAPROWS = 2 * HALF
OWN = 40
EDGE = 8
TOP = 8
EXT = ROWS + 2 * EDGE
PERMITS = (1.0, 2.1, 4.0, 12.1)
MAPS = 3
TABLE = 112
LEAD = 8
PITCH = 9
STRIPS = NMAP // 128
GROUPS = ROWS_DEV // 8
SLOTS = 4
CHIPS = SLABS // 2
PHASES = ((0, 0, 24), (SLABS * 24, 24, 16))


def split_numpy(table):
    high = table.astype(jnp.bfloat16)
    low = (table - high.astype(np.float64)).astype(jnp.bfloat16)
    return high, low


def column_table():
    freq = np.arange(HARM)[:, None]
    angle = 2.0 * np.pi * (freq * np.arange(NMAP)[None, :] % NMAP) / NMAP
    table = np.zeros((MAPROWS, NMAP))
    table[:HARM] = np.cos(angle)
    table[HALF : HALF + HARM] = -np.sin(angle)
    return np.concatenate(split_numpy(table))


def row_table():
    freq = np.arange(HARM)[None, :]
    angle = 2.0 * np.pi * (freq * np.arange(NMAP)[:, None] % NMAP) / NMAP
    table = np.zeros((NMAP, 256))
    table[:, :HARM] = np.cos(angle)
    table[:, 128 : 128 + HARM] = np.sin(angle)
    return np.stack(split_numpy(table / float(NMAP * NMAP)))


def split(value):
    high = value.astype(jnp.bfloat16)
    low = (value - high.astype(jnp.float32)).astype(jnp.bfloat16)
    return high, low


def dot_f32(a, b, contract):
    return lax.dot_general(a, b, (contract, ((), ())), preferred_element_type=jnp.float32)


def by_label(labels, values):
    low = jnp.where(labels == 0, jnp.float32(values[0]), jnp.float32(values[1]))
    high = jnp.where(labels == 2, jnp.float32(values[2]), jnp.float32(values[3]))
    return jnp.where(labels < 2, low, high)


def spectrum_kernel(
    labels_ref, col_hbm, row_hbm, out_ref, ext, smooth_a, smooth_b, fields, spec, gathered, col_ref, row_ref,
    load_sem, edge_send, edge_recv, spec_send, spec_recv, own_send, own_recv,
):
    me = lax.axis_index("slab")
    before = lax.rem(me + SLABS - 1, SLABS)
    after = lax.rem(me + 1, SLABS)

    load = pltpu.make_async_copy(labels_ref, ext.at[pl.ds(EDGE, ROWS)], load_sem.at[0])
    load.start()
    load_col = pltpu.make_async_copy(col_hbm, col_ref, load_sem.at[1])
    load_row = pltpu.make_async_copy(row_hbm, row_ref, load_sem.at[2])

    barrier = pltpu.get_barrier_semaphore()
    for step in range(1, SLABS):
        pl.semaphore_signal(barrier, inc=1, device_id={"slab": lax.rem(me + step, SLABS)})
    pl.semaphore_wait(barrier, SLABS - 1)

    up = pltpu.make_async_remote_copy(
        labels_ref.at[pl.ds(0, EDGE)], ext.at[pl.ds(EDGE + ROWS, EDGE)],
        edge_send.at[0], edge_recv.at[0], device_id={"slab": before},
    )
    down = pltpu.make_async_remote_copy(
        labels_ref.at[pl.ds(ROWS - EDGE, EDGE)], ext.at[pl.ds(0, EDGE)],
        edge_send.at[1], edge_recv.at[1], device_id={"slab": after},
    )
    up.start()
    down.start()
    load_col.start()
    load_row.start()

    def over_tiles(body, count, skip_at=None, skip=0, first=0):
        def step(i, carry):
            body(first + i if skip_at is None else first + i + jnp.where(i >= skip_at, skip, 0))
            return carry

        lax.fori_loop(0, count, step, 0)

    def to_permit(tile):
        r = pl.multiple_of(8 * tile, 8)
        for j in range(STRIPS):
            smooth_a[j, pl.ds(TOP + r, 8), :] = by_label(ext[pl.ds(r, 8), 128 * j : 128 * (j + 1)], PERMITS)

    def sides(mid, rows):
        lane = lax.broadcasted_iota(jnp.int32, (STRIPS, rows, 128), 2)
        flat = mid.reshape(STRIPS * rows, 128)
        ahead = pltpu.roll(flat, 127, 1).reshape(STRIPS, rows, 128)
        behind = pltpu.roll(flat, 1, 1).reshape(STRIPS, rows, 128)
        ahead = jnp.where(lane == 127, jnp.concatenate([ahead[1:], ahead[:1]], axis=0), ahead)
        behind = jnp.where(lane == 0, jnp.concatenate([behind[-1:], behind[:-1]], axis=0), behind)
        return behind, ahead

    def smooth_tile(src, dst):
        def body(tile):
            r = pl.multiple_of(TOP + 8 * tile, 8)
            mid = src[:, pl.ds(r, 8), :]
            behind, ahead = sides(mid, 8)
            around = src[:, pl.ds(r - 1, 8), :] + src[:, pl.ds(r + 1, 8), :] + behind + ahead
            dst[:, pl.ds(r, 8), :] = 0.5 * mid + 0.125 * around

        return body

    contrasts = [p - 1.0 / p for p in PERMITS]

    def make_fields(block):
        r = pl.multiple_of(16 * block, 16)
        at = pl.multiple_of(TOP + EDGE + r, 8)
        behind, ahead = sides(smooth_b[:, pl.ds(at, 16), :], 16)
        grad_x = 0.5 * (smooth_b[:, pl.ds(at + 1, 16), :] - smooth_b[:, pl.ds(at - 1, 16), :])
        grad_y = 0.5 * (ahead - behind)
        for j in range(STRIPS):
            lanes = slice(128 * j, 128 * (j + 1))
            labels = ext[pl.ds(pl.multiple_of(EDGE + r, 8), 16), lanes]
            permit = by_label(labels, PERMITS)
            gx, gy = grad_x[j], grad_y[j]
            factor = by_label(labels, contrasts) / (gx * gx + gy * gy + 1.0)
            along_x = factor * gx
            maps = (along_x * gy, permit - factor * gy * gy, along_x * gx - permit)
            for k in range(MAPS):
                high, low = split(maps[k])
                fields[k, 0, pl.ds(r, 16), lanes] = high
                fields[k, 1, pl.ds(r, 16), lanes] = low

    load.wait()
    over_tiles(to_permit, 16, first=1)
    over_tiles(smooth_tile(smooth_a, smooth_b), 14, first=2)
    over_tiles(smooth_tile(smooth_b, smooth_a), 12, first=3)
    over_tiles(smooth_tile(smooth_a, smooth_b), 10, first=4)
    over_tiles(make_fields, 4, first=2)
    up.wait()
    down.wait()
    over_tiles(to_permit, 2, 1, 16)
    over_tiles(smooth_tile(smooth_a, smooth_b), 4, 2, 14)
    over_tiles(smooth_tile(smooth_b, smooth_a), 6, 3, 12)
    over_tiles(smooth_tile(smooth_a, smooth_b), 8, 4, 10)
    over_tiles(make_fields, 4, 2, 4)

    def spec_copy(phase, step):
        to = lax.rem(me + step, SLABS)
        base, first, count = PHASES[phase]
        return pltpu.make_async_remote_copy(
            spec.at[pl.ds(pl.multiple_of(base + to * count, 8), count)],
            gathered.at[pl.ds(first, count), pl.ds(pl.multiple_of(me * ROWS, 128), ROWS)],
            spec_send.at[phase, step], spec_recv.at[phase, step], device_id={"slab": to},
        )

    def send_spec(phase):
        for step in range(1, SLABS):
            spec_copy(phase, step).start()
        base, first, count = PHASES[phase]
        mine = spec[pl.ds(pl.multiple_of(base + me * count, 8), count), :]
        gathered[first : first + count, pl.ds(pl.multiple_of(me * ROWS, 128), ROWS)] = mine

    load_col.wait()
    spec[MAPROWS * MAPS :, :] = jnp.zeros((SLABS * OWN - MAPROWS * MAPS, ROWS), jnp.float32)
    for k in range(MAPS):
        product = dot_f32(col_ref[...], fields[k].reshape(2 * ROWS, NMAP), ((1,), (1,)))
        half = product[:, :ROWS] + product[:, ROWS:]
        spec[MAPROWS * k : MAPROWS * (k + 1), :] = half[:MAPROWS] + half[MAPROWS:]
        if k > 0:
            send_spec(k - 1)

    core = lax.rem(me, 2)
    chip = lax.div(me, 2)

    def own_copies(phase):
        base, _, count = PHASES[phase]

        def ship(slot, origin, to, sibling=False, first=0, size=count):
            start = base + (2 * lax.rem(chip + origin + CHIPS, CHIPS) + core) * count + first
            rows = out_ref.at[pl.ds(pl.multiple_of(start, 8), size)]
            target = me + 1 - 2 * core if sibling else 2 * lax.rem(chip + to + CHIPS, CHIPS) + core
            return pltpu.make_async_remote_copy(
                rows, rows, own_send.at[phase, slot], own_recv.at[phase, slot], device_id={"slab": target}
            )

        up_part, down_part = dict(first=0, size=count - 8), dict(first=count - 8, size=8)
        chips = [ship(0, 0, 2), ship(1, 0, -2), ship(2, 0, 1), ship(3, 0, -1),
                 ship(4, -2, 2, **up_part), ship(5, 2, -2, **down_part), ship(6, -2, 1), ship(7, 2, -1)]
        siblings = [ship(8, -2, 0, True), ship(9, 2, 0, True), ship(10, -1, 0, True), ship(11, 1, 0, True),
                    ship(12, 4, 0, True, **up_part), ship(13, 4, 0, True, **down_part),
                    ship(14, -3, 0, True), ship(15, 3, 0, True), ship(16, 0, 0, True)]
        return chips, siblings

    load_row.wait()
    contract = ((1,), (0,))
    chips, siblings = zip(*(own_copies(phase) for phase in range(2)))
    for phase, (base, first, count) in enumerate(PHASES):
        for step in range(1, SLABS):
            spec_copy(phase, step).wait_recv()
        high, low = split(gathered[first : first + count, :])
        out_ref[pl.ds(pl.multiple_of(base + me * count, 8), count), :] = (
            dot_f32(high, row_ref[0], contract) + dot_f32(low, row_ref[0], contract) + dot_f32(high, row_ref[1], contract)
        )
        for i in range(4):
            chips[phase][i].start()
        siblings[phase][8].start()
    for phase in range(2):
        for i in range(2):
            chips[phase][i].wait_recv()
            chips[phase][4 + i].start()
            chips[phase][6 + i].start()
            siblings[phase][i].start()
        for i in range(2, 4):
            chips[phase][i].wait_recv()
            siblings[phase][i].start()
    for phase in range(2):
        for i in range(4, 8):
            chips[phase][i].wait_recv()
            siblings[phase][i].start()
    for phase in range(2):
        for step in range(1, SLABS):
            spec_copy(phase, step).wait_send()
        for copy in chips[phase]:
            copy.wait_send()
        for copy in siblings[phase]:
            copy.wait()


def spectrum(labels, col, row):
    vmem = pl.BlockSpec(memory_space=pltpu.VMEM)
    hbm = pl.BlockSpec(memory_space=pltpu.HBM)
    return pl.pallas_call(
        spectrum_kernel,
        out_shape=jax.ShapeDtypeStruct((SLABS * OWN, 256), jnp.float32),
        in_specs=[hbm, hbm, hbm],
        out_specs=vmem,
        scratch_shapes=[
            pltpu.VMEM((EXT, NMAP), jnp.int32),
            pltpu.VMEM((STRIPS, EXT + 2 * TOP, 128), jnp.float32),
            pltpu.VMEM((STRIPS, EXT + 2 * TOP, 128), jnp.float32),
            pltpu.VMEM((MAPS, 2, ROWS, NMAP), jnp.bfloat16),
            pltpu.VMEM((SLABS * OWN, ROWS), jnp.float32),
            pltpu.VMEM((OWN, NMAP), jnp.float32),
            pltpu.VMEM((2 * MAPROWS, NMAP), jnp.bfloat16),
            pltpu.VMEM((2, NMAP, 256), jnp.bfloat16),
            pltpu.SemaphoreType.DMA((3,)),
            pltpu.SemaphoreType.DMA((2,)),
            pltpu.SemaphoreType.DMA((2,)),
            pltpu.SemaphoreType.DMA((2, SLABS)),
            pltpu.SemaphoreType.DMA((2, SLABS)),
            pltpu.SemaphoreType.DMA((2, 17)),
            pltpu.SemaphoreType.DMA((2, 17)),
        ],
        compiler_params=pltpu.CompilerParams(
            collective_id=0, has_side_effects=True, vmem_limit_bytes=54016 * 1024
        ),
        name="spectrum",
    )(labels, col, row)


def sign_of(value):
    return jnp.where(value > 0, 1.0, jnp.where(value < 0, -1.0, 0.0))


def build_kernel(spec_ref, out_ref, toeplitz, windows_a, windows_b, stage, sem):
    first_order = lax.axis_index("slab") * (ROWS_DEV // 2)
    p_last = (first_order + ROWS_DEV // 2 - 1) * SPACING // HARM

    row = lax.broadcasted_iota(jnp.int32, (2 * TABLE, 256), 0)
    lane = lax.broadcasted_iota(jnp.int32, (2 * TABLE, 256), 1)
    m = p_last - jnp.where(row < TABLE, row, row - TABLE)
    from_cos = jnp.where(lane == jnp.abs(m), 1.0, 0.0)
    from_sin = jnp.where(lane == 128 + jnp.abs(m), sign_of(m), 0.0)
    pick = jnp.where(row < TABLE, from_cos, from_sin).astype(jnp.bfloat16)
    row = lax.broadcasted_iota(jnp.int32, (MAPROWS, 512), 0)
    lane = lax.broadcasted_iota(jnp.int32, (MAPROWS, 512), 1)
    n = HARM - 1 - (lane & 255)
    size = jnp.where(n >= 1 - HARM, jnp.abs(n), MAPROWS)
    even = jnp.where(row == size, 1.0, 0.0)
    uneven = jnp.where(row - HALF == size, sign_of(n), 0.0)
    mirror = jnp.where(lane < 256, even, uneven).astype(jnp.bfloat16)
    for k in range(MAPS):
        high, low = split(spec_ref[MAPROWS * k : MAPROWS * (k + 1), :])
        high, low = split(dot_f32(pick, high, ((1,), (1,))) + dot_f32(pick, low, ((1,), (1,))))
        product = dot_f32(high, mirror, ((1,), (0,))) + dot_f32(low, mirror, ((1,), (0,)))
        cos_rows, sin_rows = product[:TABLE], product[TABLE:]
        real = cos_rows[:, :256] + sin_rows[:, 256:]
        imag = cos_rows[:, 256:] - sin_rows[:, :256]
        for part, value in enumerate((real, imag)):
            rows = pl.ds((part * MAPS + k) * TABLE, TABLE)
            toeplitz[rows, :256], toeplitz[rows, 256:] = split(value)

    def shift_pair(group, pair):
        row = lax.broadcasted_iota(jnp.int32, (256, 256), 0)
        lane = lax.broadcasted_iota(jnp.int32, (256, 256), 1)
        orders = [(first_order + 4 * group + 2 * pair + j) * SPACING for j in range(2)]
        p_pair = [order // HARM for order in orders]
        q_pair = [order - p * HARM for order, p in zip(orders, p_pair)]
        source = jnp.where(lane < 128, lane - q_pair[0], lane - 128 - q_pair[1]) + HARM - 1
        shift = jnp.where(row == source, 1.0, 0.0).astype(jnp.bfloat16)
        shift = jnp.concatenate([shift, shift], axis=0)
        return p_pair, shift

    def make_windows(windows, p_pair, shift, pair, part):
        moved = dot_f32(toeplitz[part * MAPS * TABLE : (part + 1) * MAPS * TABLE, :], shift, ((1,), (0,)))
        for j in range(2):
            top = (LEAD - (p_last - p_pair[j])) * PITCH + 4 * pair + 2 * j
            cross_xy, right_up, left_low = (
                moved[k * TABLE : (k + 1) * TABLE, 128 * j : 128 * j + 128] for k in range(MAPS)
            )
            upper = pl.ds(top, TABLE, stride=PITCH)
            lower = pl.ds(top + 1, TABLE, stride=PITCH)
            windows[part, 0, upper, :] = cross_xy
            windows[part, 0, lower, :] = left_low
            windows[part, 1, upper, :] = right_up
            windows[part, 1, lower, :] = -cross_xy

    lane = lax.broadcasted_iota(jnp.int32, (8, 128), 1)
    sub = lax.broadcasted_iota(jnp.int32, (8, 128), 0)

    def emit(windows, slot, part, current, segments):
        for k in segments:
            half, p_j = divmod(k, HARM)
            tile, start = divmod(HARM * k, 128)
            segment = windows[part, half, (LEAD + p_j) * PITCH : (LEAD + p_j) * PITCH + 8, :]
            if start:
                segment = pltpu.roll(segment, start, 1)
                merged = jnp.where(lane < start, current, segment)
            else:
                merged = segment
            if start + HARM >= 128:
                stage[slot, part, :, 128 * tile : 128 * tile + 128] = merged
                current = segment
            else:
                current = merged
        if segments[-1] == 2 * HARM - 1:
            last = 2 * ORDERS // 128 * 128
            stage[slot, part, :, last:] = current[:, : 2 * ORDERS - last]
        return current

    def add_waves(group, slot):
        t0 = first_order + 4 * group
        order = (t0 + sub // 2) * SPACING
        p0 = t0 * SPACING // HARM
        p = jnp.where(order >= (p0 + 1) * HARM, p0 + 1, p0)
        q = order - p * HARM
        upper = sub % 2 == 0
        kx = 0.3 + 0.02 * (p - HARM // 2).astype(jnp.float32)
        ky = 0.2 + 0.02 * (q - HARM // 2).astype(jnp.float32)
        for half in range(2):
            if half == 0:
                wave = jnp.where(upper, kx * ky, ky * ky)
            else:
                wave = -jnp.where(upper, kx * kx, kx * ky)
            column = (t0 * SPACING + half * ORDERS) // 128 * 128
            place = order + half * ORDERS - column
            for j in range(2):
                lanes = pl.ds(pl.multiple_of(column + 128 * j, 128), 128)
                stage[slot, 0, :, lanes] = stage[slot, 0, :, lanes] + jnp.where(place == lane + 128 * j, wave, 0.0)

    def write(group, slot, part):
        rows = pl.ds(pl.multiple_of(8 * group, 8), 8)
        return pltpu.make_async_copy(stage.at[slot, part], out_ref.at[part, rows], sem.at[slot, part])

    for pair in range(2):
        p_pair, shift = shift_pair(0, pair)
        for part in range(2):
            make_windows(windows_a, p_pair, shift, pair, part)

    middle = HARM

    def two_groups(step, carry):
        for parity, (here, there) in enumerate(((windows_a, windows_b), (windows_b, windows_a))):
            group = 2 * step + parity
            slot = lax.rem(group, SLOTS)
            following = jnp.minimum(group + 1, GROUPS - 1)

            @pl.when(group >= SLOTS)
            def drain():
                for part in range(2):
                    write(group - SLOTS, slot, part).wait()

            for part in range(2):
                p_pair, shift = shift_pair(following, part)
                make_windows(there, p_pair, shift, part, 0)
                current = emit(here, slot, part, None, range(middle))
                make_windows(there, p_pair, shift, part, 1)
                emit(here, slot, part, current, range(middle, 2 * HARM))
                if part == 0:
                    add_waves(group, slot)
                write(group, slot, part).start()
        return carry

    lax.fori_loop(0, GROUPS // 2, two_groups, 0)
    for group in range(GROUPS - SLOTS, GROUPS):
        for part in range(2):
            write(group, group % SLOTS, part).wait()


def build(spec):
    return pl.pallas_call(
        build_kernel,
        out_shape=jax.ShapeDtypeStruct((2, ROWS_DEV, 2 * ORDERS), jnp.float32),
        in_specs=[pl.BlockSpec(memory_space=pltpu.VMEM)],
        out_specs=pl.BlockSpec(memory_space=pltpu.HBM),
        scratch_shapes=[
            pltpu.VMEM((2 * MAPS * TABLE, 512), jnp.bfloat16),
            pltpu.VMEM((2, 2, (LEAD + TABLE) * PITCH, 128), jnp.float32),
            pltpu.VMEM((2, 2, (LEAD + TABLE) * PITCH, 128), jnp.float32),
            pltpu.VMEM((SLOTS, 2, 8, 2 * ORDERS), jnp.float32),
            pltpu.SemaphoreType.DMA((SLOTS, 2)),
        ],
        compiler_params=pltpu.CompilerParams(vmem_limit_bytes=32 * 1024 * 1024),
        name="build",
    )(spec)


def shards(labels):
    spec = spectrum(labels, jnp.asarray(column_table()), jnp.asarray(row_table()))
    return build(spec)


def solution(mesh):
    return jax.shard_map(
        shards,
        mesh=mesh,
        in_specs=(P(("layer", "slab"), None),),
        out_specs=P(None, ("layer", "slab"), None),
        check_vma=False,
    )
```

time: 52.1 us -> 46.4 us (0.89)
  Pallas kernels: 52 us -> 46.4 us
    pallas_call x1, Pallas kernels: 12.2 us -> 7.65 us  [build(): pl.pallas_call(build_kernel, out_shape=jax.ShapeDtypeStruct((2, ROWS_DEV,...]
    pallas_call x1, Pallas kernels: 39.7 us -> 38.7 us  [spectrum(): pl.pallas_call(spectrum_kernel, out_shape=jax.ShapeDtypeStruct((SLABS * O...]
where the time goes in v3:
time: 46.4 us
  Pallas kernels  46.4 us (100%)
    pallas_call x1, Pallas kernels, spectrum(): pl.pallas_call(spectrum_kernel, out_shape=jax.ShapeDtypeStruct((SLABS * O...  38.7 us
    pallas_call x1, Pallas kernels, build(): pl.pallas_call(build_kernel, out_shape=jax.ShapeDtypeStruct((2, ROWS_DEV,...  7.65 us

profile of v3, /device:TPU:1, one launch (start us, length us, event | category | flops | bytes accessed | tf_op | source)
XLA Modules:
  0.0 46.4 jit_solution(6024011645566112755)
XLA Ops:
  0.0 38.7 %spectrum.1.spec_ref = f32[640,256]{1,0:T(8,128)S(1)} custom-call(s32[128,2048]{1,0:T(8,128)} %labels_ref.1, bf16[416,2048]{1,0:T(8,128)(2,1)} %constant.4.clone.col_hbm, bf16[2,2048,256]{2,1,0:T(8,128)(2,1)} %constant.5.clone.row_hbm), custom_call_target="tpu_custom_call" | custom-call | tf_op jit(solution)/shard_map/spectrum/pallas_call | solution.py:256
  38.7 7.7 %build.1 = f32[2,64,20402]{2,1,0:T(8,128)} custom-call(f32[640,256]{1,0:T(8,128)S(1)} %spectrum.1.spec_ref), custom_call_target="tpu_custom_call" | custom-call | tf_op jit(solution)/shard_map/build/pallas_call | solution.py:425

commit v4 on v3

--- a/solution.py
+++ b/solution.py
@@ -178,7 +178,7 @@
         )
 
     def send_spec(phase):
-        for step in range(1, SLABS):
+        for step in sorted(range(1, SLABS), key=lambda step: abs(step - CHIPS)):
             spec_copy(phase, step).start()
         base, first, count = PHASES[phase]
         mine = spec[pl.ds(pl.multiple_of(base + me * count, 8), count), :]
@@ -207,12 +207,8 @@
                 rows, rows, own_send.at[phase, slot], own_recv.at[phase, slot], device_id={"slab": target}
             )
 
-        up_part, down_part = dict(first=0, size=count - 8), dict(first=count - 8, size=8)
-        chips = [ship(0, 0, 2), ship(1, 0, -2), ship(2, 0, 1), ship(3, 0, -1),
-                 ship(4, -2, 2, **up_part), ship(5, 2, -2, **down_part), ship(6, -2, 1), ship(7, 2, -1)]
-        siblings = [ship(8, -2, 0, True), ship(9, 2, 0, True), ship(10, -1, 0, True), ship(11, 1, 0, True),
-                    ship(12, 4, 0, True, **up_part), ship(13, 4, 0, True, **down_part),
-                    ship(14, -3, 0, True), ship(15, 3, 0, True), ship(16, 0, 0, True)]
+        chips = [ship(i, 0, to) for i, to in enumerate((4, 3, -3, 2, -2, 1, -1))]
+        siblings = [ship(7, 0, 0, True)] + [ship(8 + i, -to, 0, True) for i, to in enumerate((4, 3, -3, 2, -2, 1, -1))]
         return chips, siblings
 
     load_row.wait()
@@ -225,22 +221,13 @@
         out_ref[pl.ds(pl.multiple_of(base + me * count, 8), count), :] = (
             dot_f32(high, row_ref[0], contract) + dot_f32(low, row_ref[0], contract) + dot_f32(high, row_ref[1], contract)
         )
-        for i in range(4):
-            chips[phase][i].start()
-        siblings[phase][8].start()
+        for copy in chips[phase]:
+            copy.start()
+        siblings[phase][0].start()
     for phase in range(2):
-        for i in range(2):
+        for i in (5, 6, 3, 4, 1, 2, 0):
             chips[phase][i].wait_recv()
-            chips[phase][4 + i].start()
-            chips[phase][6 + i].start()
-            siblings[phase][i].start()
-        for i in range(2, 4):
-            chips[phase][i].wait_recv()
-            siblings[phase][i].start()
-    for phase in range(2):
-        for i in range(4, 8):
-            chips[phase][i].wait_recv()
-            siblings[phase][i].start()
+            siblings[phase][1 + i].start()
     for phase in range(2):
         for step in range(1, SLABS):
             spec_copy(phase, step).wait_send()
@@ -272,8 +259,8 @@
             pltpu.SemaphoreType.DMA((2,)),
             pltpu.SemaphoreType.DMA((2, SLABS)),
             pltpu.SemaphoreType.DMA((2, SLABS)),
-            pltpu.SemaphoreType.DMA((2, 17)),
-            pltpu.SemaphoreType.DMA((2, 17)),
+            pltpu.SemaphoreType.DMA((2, SLABS)),
+            pltpu.SemaphoreType.DMA((2, SLABS)),
         ],
         compiler_params=pltpu.CompilerParams(
             collective_id=0, has_side_effects=True, vmem_limit_bytes=54016 * 1024

time: 46.4 us -> 46 us (level)
  Pallas kernels: 46.4 us -> 45.9 us
where the time goes in v4:
time: 46 us
  Pallas kernels  45.9 us (100%)
    pallas_call x1, Pallas kernels, spectrum(): pl.pallas_call(spectrum_kernel, out_shape=jax.ShapeDtypeStruct((SLABS * O...  38.3 us
    pallas_call x1, Pallas kernels, build(): pl.pallas_call(build_kernel, out_shape=jax.ShapeDtypeStruct((2, ROWS_DEV,...  7.65 us

profile of v4, /device:TPU:1, one launch (start us, length us, event | category | flops | bytes accessed | tf_op | source)
XLA Modules:
  0.0 46.0 jit_solution(5059776727080270580)
XLA Ops:
  0.0 38.3 %spectrum.1.spec_ref = f32[640,256]{1,0:T(8,128)S(1)} custom-call(s32[128,2048]{1,0:T(8,128)} %labels_ref.1, bf16[416,2048]{1,0:T(8,128)(2,1)} %constant.4.clone.col_hbm, bf16[2,2048,256]{2,1,0:T(8,128)(2,1)} %constant.5.clone.row_hbm), custom_call_target="tpu_custom_call" | custom-call | tf_op jit(solution)/shard_map/spectrum/pallas_call | solution.py:243
  38.3 7.6 %build.1 = f32[2,64,20402]{2,1,0:T(8,128)} custom-call(f32[640,256]{1,0:T(8,128)S(1)} %spectrum.1.spec_ref), custom_call_target="tpu_custom_call" | custom-call | tf_op jit(solution)/shard_map/build/pallas_call | solution.py:412

commit v5 on v4

--- a/solution.py
+++ b/solution.py
@@ -107,7 +107,7 @@
             body(first + i if skip_at is None else first + i + jnp.where(i >= skip_at, skip, 0))
             return carry
 
-        lax.fori_loop(0, count, step, 0)
+        lax.fori_loop(0, count, step, 0, unroll=2 if body is make_fields else count // 2)
 
     def to_permit(tile):
         r = pl.multiple_of(8 * tile, 8)

time: 46 us -> 42.4 us (0.922)
  Pallas kernels: 45.9 us -> 42.4 us
    pallas_call x1, Pallas kernels: 38.3 us -> 34.7 us  [spectrum(): pl.pallas_call(spectrum_kernel, out_shape=jax.ShapeDtypeStruct((SLABS * O...]
where the time goes in v5:
time: 42.4 us
  Pallas kernels  42.4 us (100%)
    pallas_call x1, Pallas kernels, spectrum(): pl.pallas_call(spectrum_kernel, out_shape=jax.ShapeDtypeStruct((SLABS * O...  34.7 us
    pallas_call x1, Pallas kernels, build(): pl.pallas_call(build_kernel, out_shape=jax.ShapeDtypeStruct((2, ROWS_DEV,...  7.65 us

profile of v5, /device:TPU:1, one launch (start us, length us, event | category | flops | bytes accessed | tf_op | source)
XLA Modules:
  0.0 42.4 jit_solution(15641953290245211751)
XLA Ops:
  0.0 34.7 %spectrum.1.spec_ref = f32[640,256]{1,0:T(8,128)S(1)} custom-call(s32[128,2048]{1,0:T(8,128)} %labels_ref.1, bf16[416,2048]{1,0:T(8,128)(2,1)} %constant.4.clone.col_hbm, bf16[2,2048,256]{2,1,0:T(8,128)(2,1)} %constant.5.clone.row_hbm), custom_call_target="tpu_custom_call" | custom-call | tf_op jit(solution)/shard_map/spectrum/pallas_call | solution.py:243
  34.7 7.7 %build.1 = f32[2,64,20402]{2,1,0:T(8,128)} custom-call(f32[640,256]{1,0:T(8,128)S(1)} %spectrum.1.spec_ref), custom_call_target="tpu_custom_call" | custom-call | tf_op jit(solution)/shard_map/build/pallas_call | solution.py:412
